TPU v7x, 32 devices: a whole 2x2x4 slice. The times are simulated.
32 devices in a mesh: gx: 4 (over x, core), gy: 8 (over z, y).
Axes of the slice: x: 2, y: 2, z: 4, core: 2. Of those that a mesh axis runs over, the one named last changes fastest.
Arguments:
- queries: bfloat16 [4096, 2048], P(('gx', 'gy')), may hold values from -100 to 100
- keys_local: bfloat16 [4096, 2048], P(('gx', 'gy')), may hold values from -5 to 5
- values_local: bfloat16 [4096, 2048], P(('gx', 'gy')), may hold values from -5 to 5
- mem_keys: bfloat16 [16384, 2048], P(('gx', 'gy')), may hold values from -5 to 5
- mem_values: bfloat16 [16384, 2048], P(('gx', 'gy')), may hold values from -5 to 5
- proj: bfloat16 [2048, 2048], P(('gx', 'gy')), may hold values from -0.125 to 0.125
- cotangent: bfloat16 [4096, 2048], P(('gx', 'gy')), may hold values from -6 to 6
- block_list: int32 [32, 16, 3], P(('gx', 'gy')), may hold values from 0 to 31, as said below
Outputs:
- mixed: bfloat16 [4096, 2048], P(('gx', 'gy'))
- grad_proj: float32 [2048, 2048], P(('gx', 'gy'))
- grad_queries: bfloat16 [4096, 2048], P(('gx', 'gy'))
- grad_keys_local: bfloat16 [4096, 2048], P(('gx', 'gy'))
- grad_values_local: bfloat16 [4096, 2048], P(('gx', 'gy'))
- grad_mem_keys: bfloat16 [16384, 2048], P(('gx', 'gy'))
- grad_mem_values: bfloat16 [16384, 2048], P(('gx', 'gy'))
Inputs may be any that keep to these rules, and one draw needn't show every extreme that they name: `block_list`: query blocks of gx index i belong to document i. Among the requests of the 1 query block of one device, exactly 8 (block, head) pairs name blocks of each of 6 of the document's memory devices and none name the others' blocks, where memory device j of the document holds its blocks j * 4 to j * 4 + 3. The 3 blocks of one query block and head are distinct.
All inputs are finite; a program needn't handle non-finite values.
Results may differ from a plain program's by a relative error of at most 0.009.
Values may be sent and summed in bfloat16 or wider, within the bound.
A program may use at most 128 MiB of HBM per device.

v0:
```python
import jax
import jax.numpy as jnp
from jax import lax
from jax.sharding import PartitionSpec as P

H = 16
DH = 128
BLK = 128
KB = 3
QB = 1
MB_DEV = 4


def split_heads(matrix):
    return matrix.reshape(QB, BLK, H, DH).transpose(0, 2, 1, 3)


def join_heads(blocks):
    return blocks.transpose(0, 2, 1, 3).reshape(QB * BLK, H * DH)


def local(queries, keys_local, values_local, mem_keys, mem_values, proj, cotangent, block_list):
    cycle_y = lax.axis_size("gy")
    cycle_x = lax.axis_size("gx")
    item_count = QB * H * KB
    capacity = item_count // (cycle_y - cycle_y // 4)
    slot_count = cycle_y * capacity
    table_rows = MB_DEV * H
    ordered = jnp.transpose(block_list, (2, 0, 1)).reshape(item_count)
    head_of = jnp.broadcast_to(jnp.arange(H, dtype=jnp.int32)[None, None, :], (KB, QB, H)).reshape(
        item_count
    )
    owners = ordered // MB_DEV
    code_list = ordered % MB_DEV * H + head_of
    owner_hot = (owners[:, None] == jnp.arange(cycle_y, dtype=jnp.int32)[None, :]).astype(jnp.int32)
    slot_of = jnp.sum(owner_hot * (jnp.cumsum(owner_hot, axis=0) - 1), axis=1)
    position = owners * capacity + slot_of
    selector = position[:, None] == jnp.arange(slot_count, dtype=jnp.int32)[None, :]
    request = jnp.sum(jnp.where(selector, code_list[:, None], 0), axis=0).reshape(cycle_y, capacity)
    key_table = mem_keys.reshape(MB_DEV, BLK, H, DH).transpose(0, 2, 1, 3)
    value_table = mem_values.reshape(MB_DEV, BLK, H, DH).transpose(0, 2, 1, 3)
    block_table = jnp.concatenate([key_table, value_table], axis=-1).reshape(
        table_rows, BLK * 2 * DH
    )
    wanted = lax.all_to_all(request, "gy", split_axis=0, concat_axis=0, tiled=True)
    count = wanted.shape[1]
    chooser = (
        wanted.reshape(-1)[:, None] == jnp.arange(table_rows, dtype=jnp.int32)[None, :]
    ).astype(jnp.bfloat16)
    found = jnp.dot(chooser, block_table, preferred_element_type=jnp.float32).astype(jnp.bfloat16)
    found = found.reshape(cycle_y, count, BLK, 2 * DH)
    returned = lax.all_to_all(found, "gy", split_axis=0, concat_axis=0, tiled=True)
    selector_bf = selector.astype(jnp.bfloat16)
    fetched = jnp.dot(
        selector_bf, returned.reshape(slot_count, BLK * 2 * DH), preferred_element_type=jnp.float32
    )
    fetched = fetched.astype(jnp.bfloat16).reshape(KB, QB, H, BLK, 2 * DH).transpose(1, 2, 0, 3, 4)
    key_mem = fetched[..., :DH].reshape(QB, H, KB * BLK, DH)
    value_mem = fetched[..., DH:].reshape(QB, H, KB * BLK, DH)
    query_blocks = split_heads(queries)
    all_keys = jnp.concatenate([split_heads(keys_local), key_mem], axis=2)
    all_values = jnp.concatenate([split_heads(values_local), value_mem], axis=2)
    score_scale = DH ** (-0.5)
    scores = (
        jnp.einsum("bhqd,bhkd->bhqk", query_blocks, all_keys, preferred_element_type=jnp.float32)
        * score_scale
    )
    column = jnp.arange(all_keys.shape[2], dtype=jnp.int32)[None, :]
    row_index = jnp.arange(BLK, dtype=jnp.int32)[:, None]
    visible = (column >= BLK) | (column <= row_index)
    scores = jnp.where(visible[None, None], scores, jnp.float32(-1e30))
    row_max = jnp.max(scores, axis=-1, keepdims=True)
    expo = jnp.exp(scores - row_max)
    probability = expo / jnp.sum(expo, axis=-1, keepdims=True)
    weights_bf = probability.astype(jnp.bfloat16)
    attended_blocks = jnp.einsum(
        "bhqk,bhkd->bhqd", weights_bf, all_values, preferred_element_type=jnp.float32
    )
    attended = join_heads(attended_blocks.astype(jnp.bfloat16))
    columns = attended
    mixed_sum = jnp.dot(
        columns,
        lax.all_gather(proj, ("gx", "gy"), axis=0, tiled=True),
        preferred_element_type=jnp.float32,
    )
    d_attended = lax.dot_general(
        cotangent,
        lax.all_gather(proj, ("gx", "gy"), axis=0, tiled=True),
        (((1,), (1,)), ((), ())),
        preferred_element_type=jnp.float32,
    )
    mixed = mixed_sum.astype(jnp.bfloat16)
    d_attended = d_attended.astype(jnp.bfloat16)
    total_tokens = queries.shape[0] * cycle_x * cycle_y
    columns = attended
    grad_sum = lax.psum_scatter(
        lax.dot_general(
            columns, cotangent, (((0,), (0,)), ((), ())), preferred_element_type=jnp.float32
        ),
        ("gx", "gy"),
        scatter_dimension=0,
        tiled=True,
    )
    grad_proj = grad_sum * total_tokens ** (-0.5)
    d_blocks = split_heads(d_attended)
    d_prob = jnp.einsum("bhqd,bhkd->bhqk", d_blocks, all_values, preferred_element_type=jnp.float32)
    delta = jnp.sum(probability * d_prob, axis=-1, keepdims=True)
    d_score = (probability * (d_prob - delta) * score_scale).astype(jnp.bfloat16)
    grad_query_blocks = jnp.einsum(
        "bhqk,bhkd->bhqd", d_score, all_keys, preferred_element_type=jnp.float32
    )
    key_terms = jnp.einsum(
        "bhqk,bhqd->bhkd", d_score, query_blocks, preferred_element_type=jnp.float32
    )
    value_terms = jnp.einsum(
        "bhqk,bhqd->bhkd", weights_bf, d_blocks, preferred_element_type=jnp.float32
    )
    grad_queries = join_heads(grad_query_blocks.astype(jnp.bfloat16))
    grad_keys_local = join_heads(key_terms[:, :, :BLK].astype(jnp.bfloat16))
    grad_values_local = join_heads(value_terms[:, :, :BLK].astype(jnp.bfloat16))
    mem_key_terms = key_terms[:, :, BLK:].astype(jnp.bfloat16).reshape(QB, H, KB, BLK, DH)
    mem_value_terms = value_terms[:, :, BLK:].astype(jnp.bfloat16).reshape(QB, H, KB, BLK, DH)
    packed = jnp.concatenate([mem_key_terms, mem_value_terms], axis=-1).transpose(2, 0, 1, 3, 4)
    packed = packed.reshape(item_count, BLK * 2 * DH)
    outgoing = lax.dot_general(
        selector_bf, packed, (((0,), (0,)), ((), ())), preferred_element_type=jnp.float32
    )
    outgoing = outgoing.astype(jnp.bfloat16).reshape(cycle_y, capacity, BLK, 2 * DH)
    incoming = lax.all_to_all(outgoing, "gy", split_axis=0, concat_axis=0, tiled=True)
    chooser = (
        wanted.reshape(-1)[:, None] == jnp.arange(table_rows, dtype=jnp.int32)[None, :]
    ).astype(jnp.bfloat16)
    table_grad = lax.dot_general(
        chooser,
        incoming.reshape(slot_count, BLK * 2 * DH),
        (((0,), (0,)), ((), ())),
        preferred_element_type=jnp.float32,
    )
    table_grad = table_grad.reshape(MB_DEV, H, BLK, 2 * DH)
    grad_mem_keys = (
        table_grad[..., :DH]
        .transpose(0, 2, 1, 3)
        .reshape(MB_DEV * BLK, H * DH)
        .astype(jnp.bfloat16)
    )
    grad_mem_values = (
        table_grad[..., DH:]
        .transpose(0, 2, 1, 3)
        .reshape(MB_DEV * BLK, H * DH)
        .astype(jnp.bfloat16)
    )
    return (
        mixed,
        grad_proj,
        grad_queries,
        grad_keys_local,
        grad_values_local,
        grad_mem_keys,
        grad_mem_values,
    )


def solution(mesh):
    return jax.shard_map(
        local,
        mesh=mesh,
        in_specs=(
            P(("gx", "gy"), None),
            P(("gx", "gy"), None),
            P(("gx", "gy"), None),
            P(("gx", "gy"), None),
            P(("gx", "gy"), None),
            P(("gx", "gy"), None),
            P(("gx", "gy"), None),
            P(("gx", "gy"), None, None),
        ),
        out_specs=(
            P(("gx", "gy"), None),
            P(("gx", "gy"), None),
            P(("gx", "gy"), None),
            P(("gx", "gy"), None),
            P(("gx", "gy"), None),
            P(("gx", "gy"), None),
            P(("gx", "gy"), None),
        ),
        check_vma=False,
    )
```

profile of v0, /device:TPU:0, one launch (start us, length us, event | category | flops | bytes accessed | tf_op | source)
XLA Modules:
  0.0 615.5 jit_solution(3434968699146197829)
XLA Ops:
  9.9 7.3 %all-to-all-start = ((s32[8,1,8]{2,1,0:T(1,128)}), s32[8,1,8]{2,1,0:T(1,128)S(1)}, u32[]{:S(2)}, u32[]{:S(2)}) async-start(s32[8,1,8]{2,1,0:T(1,128)} %bitcast.3), calls=%async_computation | async-start | bytes 8192 | tf_op jit(solution)/shard_map/all_to_all | solution.py:45
  17.2 2.2 copy.106
  21.9 4.6 copy.108
  27.8 5.4 convolution_convert_fusion.1
  33.2 6.1 all-to-all-start.1
  41.3 124.7 %all-to-all-done.1 = bf16[8,8,128,256]{3,1,2,0:T(8,128)(2,1)} async-done(((bf16[8,8,128,256]{3,1,2,0:T(8,128)(2,1)}), bf16[8,8,128,256]{3,1,2,0:T(8,128)(2,1)}, u32[]{:S(2)}, u32[]{:S(2)}) %all-to-all-start.1) | async-done | bytes 4194336 | tf_op jit(solution)/shard_map/all_to_all | solution.py:52
  166.0 3.2 convolution_convert_fusion.2
  170.3 2.0 fusion.62
  173.9 2.1 fusion.22
  179.7 8.1 %fusion.64 = f32[2048,2048]{1,0:T(8,128)} fusion(bf16[128,2048]{0,1:T(8,128)(2,1)S(1)} %bitcast.167, bf16[128,2048]{1,0:T(8,128)(2,1)S(1)} %copy-done), kind=kOutput, calls=%fused_computation.94 | convolution fusion | flops 1073741824 | bytes 17825792 | tf_op jit(solution)/shard_map/dot_general | solution.py:97
  187.9 6.4 %fusion.29 = bf16[16,8,16,128]{3,1,2,0:T(8,128)(2,1)S(1)} fusion(bf16[128,2048]{1,0:T(8,128)(2,1)S(1)} %copy-done, bf16[2048,2048]{1,0:T(8,128)(2,1)} %all-gather.2.cloned.1.call-done), kind=kOutput, calls=%fused_computation.41 | convolution fusion | flops 1074003968 | bytes 9437184 | tf_op jit(solution)/shard_map/dot_general | solution.py:86
  195.5 1.9 copy-done.5
  197.4 2.7 fusion.23
  200.1 8.8 %convert_bitcast_fusion.1 = bf16[1,16,512,128]{3,2,1,0:T(8,128)(2,1)} fusion(f32[16,128,512]{1,2,0:T(8,128)} %fusion.23, bf16[1,128,16,128]{3,2,1,0:T(8,128)(2,1)S(1)} %bitcast.179, f32[16,128,512]{1,2,0:T(8,128)} %copy-done.16, f32[16,128]{1,0:T(8,128)S(1)} %get-tuple-element.41), kind=kOutput, calls=%fused_computation.29 | convolution fusion | flops 276826624 | bytes 11018240 | tf_op jit(solution)/shard_map/bhqk,bhqd->bhkd/dot_general | solution.py:112
  211.6 2.1 copy.112
  213.7 3.4 convolution_convert_fusion
  217.1 4.7 all-to-all-start.2
  221.9 9.2 %fusion.25 = bf16[16,128,128]{1,2,0:T(8,128)(2,1)} fusion(bf16[1,16,384,128]{3,2,1,0:T(8,128)(2,1)} %bitcast.166, bf16[1,16,128,128]{3,2,1,0:T(8,128)(2,1)S(1)} %bitcast.177, f32[16,128,512]{1,2,0:T(8,128)} %fusion.23, f32[16,128,512]{1,2,0:T(8,128)} %copy-done.16, f32[16,128]{1,0:T(8,128)S(1)} %get-tuple-element.41), kind=kOutput, calls=%fused_computation.39 | convolution fusion | flops 280234496 | bytes 11018240 | tf_op jit(solution)/shard_map/bhqk,bhkd->bhqd/dot_general | solution.py:109
  231.1 2.0 copy.95
  236.9 5.5 convolution_convert_fusion.4
  242.3 98.7 %all-to-all-done.2 = bf16[8,8,128,256]{3,1,2,0:T(8,128)(2,1)} async-done(((bf16[8,8,128,256]{3,1,2,0:T(8,128)(2,1)}), bf16[8,8,128,256]{3,1,2,0:T(8,128)(2,1)}, u32[]{:S(2)}, u32[]{:S(2)}) %all-to-all-start.2) | async-done | bytes 4194336 | tf_op jit(solution)/shard_map/all_to_all | solution.py:129
  341.0 3.5 fusion.8
  349.1 257.7 %reduce-scatter.2.cloned.1.call-done = f32[64,2048]{1,0:T(8,128)} async-done(((f32[2048,2048]{1,0:T(8,128)}), f32[64,2048]{1,0:T(8,128)}) %reduce-scatter.2.cloned.1.call-update) | async-done | bytes 524304 | tf_op jit(solution)/shard_map/reduce_scatter | solution.py:96
  606.7 1.9 broadcast_multiply_fusion
  (87 shorter events, 26.7 us)
Async XLA Ops:
  7.2 172.6 %copy-start = (bf16[128,2048]{1,0:T(8,128)(2,1)S(1)}, bf16[128,2048]{1,0:T(8,128)(2,1)}, u32[]{:S(2)}) copy-start(bf16[128,2048]{1,0:T(8,128)(2,1)} %param.14) | copy-start | bytes 1572868
  7.2 12.3 %copy-start.6 = (bf16[512,2048]{1,0:T(8,128)(2,1)S(1)}, bf16[512,2048]{1,0:T(8,128)(2,1)}, u32[]{:S(2)}) copy-start(bf16[512,2048]{1,0:T(8,128)(2,1)} %param.12) | copy-start | bytes 6291460
  7.2 180.7 %all-gather.2.cloned.1.call-start = ((), (), s32[]{:S(2)}) async-start(), calls=%async_computation.4 | async-start | bytes 8650752 | tf_op jit(solution)/shard_map/all_gather | solution.py:83
  9.9 16.6 %all-to-all-start = ((s32[8,1,8]{2,1,0:T(1,128)}), s32[8,1,8]{2,1,0:T(1,128)S(1)}, u32[]{:S(2)}, u32[]{:S(2)}) async-start(s32[8,1,8]{2,1,0:T(1,128)} %bitcast.3), calls=%async_computation | async-start | bytes 8192 | tf_op jit(solution)/shard_map/all_to_all | solution.py:45
  33.2 6.2 %copy-start.13 = (bf16[128,2048]{1,0:T(8,128)(2,1)S(1)}, bf16[128,2048]{1,0:T(8,128)(2,1)}, u32[]{:S(2)}) copy-start(bf16[128,2048]{1,0:T(8,128)(2,1)} %param.8) | copy-start | bytes 1572868
  33.2 6.3 %copy-start.14 = (bf16[128,2048]{1,0:T(8,128)(2,1)S(1)}, bf16[128,2048]{1,0:T(8,128)(2,1)}, u32[]{:S(2)}) copy-start(bf16[128,2048]{1,0:T(8,128)(2,1)} %param.9) | copy-start | bytes 1572868
  33.2 6.9 %copy-start.15 = (bf16[128,2048]{1,0:T(8,128)(2,1)S(1)}, bf16[128,2048]{1,0:T(8,128)(2,1)}, u32[]{:S(2)}) copy-start(bf16[128,2048]{1,0:T(8,128)(2,1)} %param.10) | copy-start | bytes 1572868
  33.2 132.8 %all-to-all-start.1 = ((bf16[8,8,128,256]{3,1,2,0:T(8,128)(2,1)}), bf16[8,8,128,256]{3,1,2,0:T(8,128)(2,1)}, u32[]{:S(2)}, u32[]{:S(2)}) async-start(bf16[8,8,128,256]{3,1,2,0:T(8,128)(2,1)} %bitcast.150), calls=%async_computation.1 | async-start | bytes 8388608 | tf_op jit(solution)/shard_map/all_to_all | solution.py:52
  39.4 567.4 %reduce-scatter.2.cloned.1.call-start = ((), (), s32[]{:S(2)}) async-start(), calls=%async_computation.5 | async-start | bytes 17301504 | tf_op jit(solution)/shard_map/reduce_scatter | solution.py:96
  39.5 134.4 %copy-start.9 = (bf16[16,8,16,128]{3,2,1,0:T(8,128)(2,1)}, bf16[16,8,16,128]{3,2,1,0:T(8,128)(2,1)S(1)}, u32[]{:S(2)}) copy-start(bf16[16,8,16,128]{3,2,1,0:T(8,128)(2,1)S(1)} %copy.110) | copy-start | bytes 1572868
  40.1 133.8 %copy-start.7 = (bf16[1,128,16,128]{3,1,2,0:T(8,128)(2,1)}, bf16[1,128,16,128]{3,1,2,0:T(8,128)(2,1)S(1)}, u32[]{:S(2)}) copy-start(bf16[1,128,16,128]{3,1,2,0:T(8,128)(2,1)S(1)} %copy.75) | copy-start | bytes 1572868
  176.0 1.7 copy-start.4
  176.1 1.7 copy-start.11
  177.8 2.0 copy-start.16
  187.9 6.6 %copy-start.17 = (f32[16,128,512]{1,2,0:T(8,128)S(1)}, f32[16,128,512]{1,2,0:T(8,128)}, u32[]{:S(2)}) copy-start(f32[16,128,512]{1,2,0:T(8,128)} %copy-done.16) | copy-start | bytes 12582916
  195.2 4.9 copy-start.2
  195.2 2.2 copy-start.5
  197.4 2.7 copy-start.10
  208.9 1.4 slice-start
  208.9 1.9 slice-start.1
  217.1 4.7 copy-start.8
  217.1 123.9 %all-to-all-start.2 = ((bf16[8,8,128,256]{3,1,2,0:T(8,128)(2,1)}), bf16[8,8,128,256]{3,1,2,0:T(8,128)(2,1)}, u32[]{:S(2)}, u32[]{:S(2)}) async-start(bf16[8,8,128,256]{3,1,2,0:T(8,128)(2,1)} %bitcast.149), calls=%async_computation.3 | async-start | bytes 8388608 | tf_op jit(solution)/shard_map/all_to_all | solution.py:129
  221.8 11.3 %copy-start.3 = (bf16[1,16,512,128]{3,2,1,0:T(8,128)(2,1)S(1)}, bf16[1,16,512,128]{3,2,1,0:T(8,128)(2,1)}, u32[]{:S(2)}) copy-start(bf16[1,16,512,128]{3,2,1,0:T(8,128)(2,1)} %copy-done.2) | copy-start | bytes 6291460
  345.4 263.3 %copy-start.1 = (bf16[128,2048]{1,0:T(8,128)(2,1)S(1)}, bf16[128,2048]{1,0:T(8,128)(2,1)}, u32[]{:S(2)}) copy-start(bf16[128,2048]{1,0:T(8,128)(2,1)} %param.14) | copy-start | bytes 1572868
  (1 other events, 1.0 us)
Sparse Core Ops, SparseCore 0:
  11.0 146.9 all-gather.1
  188.0 418.7 reduce-scatter.1
where the time goes:
time: 616 us; the launch traced here: 615 us
  waiting for transfers between devices  482 us (78%)
  matrix products  59.8 us (10%)
  local copies, waits for them, and re-layouts  35.3 us (6%)
  starting transfers between devices  18.2 us (3%)
  between operations  14.4 us (2%)
    reduce_scatter x1, waiting for transfers between devices, local(): lax.psum_scatter(lax.dot_general(columns, cotangent, (((0,), (0,)), ((),...  258 us
    all_to_all x1, waiting for transfers between devices, local(): lax.all_to_all(found, 'gy', split_axis=0, concat_axis=0, tiled=True)  125 us
    all_to_all x1, waiting for transfers between devices, local(): lax.all_to_all(outgoing, 'gy', split_axis=0, concat_axis=0, tiled=True)  98.7 us
    unnamed x50, local copies, waits for them, and re-layouts  23.1 us
  transfers between devices with their start and end apart: 5, of which 3 were waited for; matrix products, arithmetic and copies ran while one was open for 15% of the time, Pallas kernels for 0%

commit v1 on v0

v1 whole, which is shorter than its diff:
```python
import functools

import jax
import jax.numpy as jnp
from jax import lax
from jax.experimental import pallas as pl
from jax.experimental.pallas import tpu as pltpu
from jax.sharding import PartitionSpec as P

H = 16
DH = 128
BLK = 128
KB = 3
MB_DEV = 4
HEADS_PER_STEP = 2
VMEM_BYTES = 48 * 1024 * 1024


def params(**extra):
    return pltpu.CompilerParams(vmem_limit_bytes=VMEM_BYTES, **extra)


def block_of(code):
    rows = pl.ds(pl.multiple_of((code // H) * BLK, BLK), BLK)
    columns = pl.ds(pl.multiple_of((code % H) * DH, DH), DH)
    return rows, columns


def gather_kernel(capacity, wanted_ref, keys_ref, values_ref, found_ref):
    base = pl.program_id(0) * capacity

    def body(slot, carry):
        rows, columns = block_of(jnp.maximum(wanted_ref[base + slot], 0))
        found_ref[slot, :, :DH] = keys_ref[rows, columns]
        found_ref[slot, :, DH:] = values_ref[rows, columns]
        return carry

    lax.fori_loop(0, capacity, body, 0)


def gather_blocks(wanted, mem_keys, mem_values, peers, capacity):
    whole = pl.BlockSpec(mem_keys.shape, lambda i, wanted: (0, 0))
    return pl.pallas_call(
        functools.partial(gather_kernel, capacity),
        out_shape=jax.ShapeDtypeStruct((peers * capacity, BLK, 2 * DH), jnp.bfloat16),
        grid_spec=pltpu.PrefetchScalarGridSpec(
            num_scalar_prefetch=1,
            grid=(peers,),
            in_specs=[whole, whole],
            out_specs=pl.BlockSpec((capacity, BLK, 2 * DH), lambda i, wanted: (i, 0, 0)),
        ),
        compiler_params=params(),
    )(wanted, mem_keys, mem_values)


def dot_nt(a, b):
    return lax.dot_general(a, b, (((1,), (1,)), ((), ())), preferred_element_type=jnp.float32)


def dot_tn(a, b):
    return lax.dot_general(a, b, (((0,), (0,)), ((), ())), preferred_element_type=jnp.float32)


def attention_kernel(
    position_ref, q_ref, k_ref, v_ref, do_ref, mem_ref, att_ref, dq_ref, dk_ref, dv_ref, out_ref
):
    scale = DH ** (-0.5)
    step = pl.program_id(0)
    column = lax.broadcasted_iota(jnp.int32, (BLK, (KB + 1) * BLK), 1)
    row = lax.broadcasted_iota(jnp.int32, (BLK, (KB + 1) * BLK), 0)
    visible = (column >= BLK) | (column <= row)
    for part in range(HEADS_PER_STEP):
        head = step * HEADS_PER_STEP + part
        here = slice(part * DH, (part + 1) * DH)
        slots = [position_ref[k * H + head] for k in range(KB)]
        q = q_ref[:, here]
        do = do_ref[:, here]
        keys = jnp.concatenate([k_ref[:, here]] + [mem_ref[s, :, :DH] for s in slots], axis=0)
        values = jnp.concatenate([v_ref[:, here]] + [mem_ref[s, :, DH:] for s in slots], axis=0)
        scores = jnp.where(visible, dot_nt(q, keys) * scale, jnp.float32(-1e30))
        expo = jnp.exp(scores - jnp.max(scores, axis=-1, keepdims=True))
        probability = expo / jnp.sum(expo, axis=-1, keepdims=True)
        weights = probability.astype(jnp.bfloat16)
        att_ref[:, here] = jnp.dot(weights, values, preferred_element_type=jnp.float32).astype(
            jnp.bfloat16
        )
        d_prob = dot_nt(do, values)
        delta = jnp.sum(probability * d_prob, axis=-1, keepdims=True)
        d_score = (probability * (d_prob - delta) * scale).astype(jnp.bfloat16)
        dq_ref[:, here] = jnp.dot(d_score, keys, preferred_element_type=jnp.float32).astype(
            jnp.bfloat16
        )
        key_terms = dot_tn(d_score, q).astype(jnp.bfloat16)
        value_terms = dot_tn(weights, do).astype(jnp.bfloat16)
        dk_ref[:, here] = key_terms[:BLK]
        dv_ref[:, here] = value_terms[:BLK]
        for k, slot in enumerate(slots):
            rows = slice((k + 1) * BLK, (k + 2) * BLK)
            out_ref[slot, :, :DH] = key_terms[rows]
            out_ref[slot, :, DH:] = value_terms[rows]


def attend(position, queries, keys_local, values_local, d_attended, returned):
    tokens, features = queries.shape
    heads = pl.BlockSpec((tokens, HEADS_PER_STEP * DH), lambda i, position: (0, i))
    whole = pl.BlockSpec(returned.shape, lambda i, position: (0, 0, 0))
    rows = jax.ShapeDtypeStruct((tokens, features), jnp.bfloat16)
    return pl.pallas_call(
        attention_kernel,
        out_shape=(rows, rows, rows, rows, jax.ShapeDtypeStruct(returned.shape, jnp.bfloat16)),
        grid_spec=pltpu.PrefetchScalarGridSpec(
            num_scalar_prefetch=1,
            grid=(H // HEADS_PER_STEP,),
            in_specs=[heads, heads, heads, heads, whole],
            out_specs=(heads, heads, heads, heads, whole),
        ),
        compiler_params=params(),
    )(position, queries, keys_local, values_local, d_attended, returned)


def collect_kernel(capacity, wanted_ref, incoming_ref, keys_ref, values_ref, key_sum, value_sum):
    step = pl.program_id(0)

    @pl.when(step == 0)
    def _():
        key_sum[...] = jnp.zeros_like(key_sum)
        value_sum[...] = jnp.zeros_like(value_sum)

    def body(slot, carry):
        code = wanted_ref[step * capacity + slot]

        @pl.when(code >= 0)
        def _():
            where = block_of(code)
            key_sum[where] += incoming_ref[slot, :, :DH].astype(jnp.float32)
            value_sum[where] += incoming_ref[slot, :, DH:].astype(jnp.float32)

        return carry

    lax.fori_loop(0, capacity, body, 0)

    @pl.when(step == pl.num_programs(0) - 1)
    def _():
        keys_ref[...] = key_sum[...].astype(jnp.bfloat16)
        values_ref[...] = value_sum[...].astype(jnp.bfloat16)


def collect_terms(wanted, incoming, peers, capacity):
    shape = (MB_DEV * BLK, H * DH)
    whole = pl.BlockSpec(shape, lambda i, wanted: (0, 0))
    table = jax.ShapeDtypeStruct(shape, jnp.bfloat16)
    return pl.pallas_call(
        functools.partial(collect_kernel, capacity),
        out_shape=(table, table),
        grid_spec=pltpu.PrefetchScalarGridSpec(
            num_scalar_prefetch=1,
            grid=(peers,),
            in_specs=[pl.BlockSpec((capacity, BLK, 2 * DH), lambda i, wanted: (i, 0, 0))],
            out_specs=(whole, whole),
            scratch_shapes=[pltpu.VMEM(shape, jnp.float32), pltpu.VMEM(shape, jnp.float32)],
        ),
        compiler_params=params(),
    )(wanted, incoming)


def projection_gradient(attended, cotangent, sizes):
    order = []
    for name in ("gx", "gy"):
        order += [(name, bit) for bit in range(sizes[name].bit_length() - 1)]
    dims = [(name, bit) for name in ("gx", "gy") for bit in reversed(range(sizes[name].bit_length() - 1))]
    tokens, features = attended.shape
    rest = features // (sizes["gx"] * sizes["gy"])
    columns = attended.reshape((tokens,) + (2,) * len(dims) + (rest,))
    total = None
    for place, (name, bit) in enumerate(order):
        axis = dims.index((name, bit))
        mine = (lax.axis_index(name) >> bit) & 1
        pairs = [(i, i ^ (1 << bit)) for i in range(sizes[name])]
        dims = dims[:axis] + dims[axis + 1 :]
        last = place == len(order) - 1
        if total is None:
            shape = (2,) * len(dims) + (rest, cotangent.shape[1])

            def product(which):
                part = lax.dynamic_index_in_dim(columns, which, axis + 1, keepdims=False)
                return dot_tn(part.reshape(tokens, features // 2), cotangent)

            sent = product(1 - mine).astype(jnp.bfloat16).reshape(shape)
            kept = product(mine).reshape(shape)
        else:
            sent = lax.dynamic_index_in_dim(total, 1 - mine, axis, keepdims=False)
            kept = lax.dynamic_index_in_dim(total, mine, axis, keepdims=False).astype(jnp.float32)
        total = kept + lax.ppermute(sent, name, pairs).astype(jnp.float32)
        if not last:
            total = total.astype(jnp.bfloat16)
    return total


def local(sizes, queries, keys_local, values_local, mem_keys, mem_values, proj, cotangent, block_list):
    peers = sizes["gy"]
    item_count = H * KB
    capacity = item_count // (peers - peers // 4)
    slot_count = peers * capacity
    ordered = block_list.reshape(H, KB).T.reshape(item_count)
    item = jnp.arange(item_count, dtype=jnp.int32)
    owners = ordered // MB_DEV
    codes = ordered % MB_DEV * H + item % H
    earlier = (owners[:, None] == owners[None, :]) & (item[None, :] < item[:, None])
    position = owners * capacity + jnp.sum(earlier.astype(jnp.int32), axis=1)
    selector = jnp.arange(slot_count, dtype=jnp.int32)[:, None] == position[None, :]
    request = jnp.sum(jnp.where(selector, codes[None, :] + 1, 0), axis=1) - 1
    wanted = lax.all_to_all(
        request.reshape(peers, capacity), "gy", split_axis=0, concat_axis=0, tiled=True
    ).reshape(slot_count)

    found = gather_blocks(wanted, mem_keys, mem_values, peers, capacity)
    returned = lax.all_to_all(
        found.reshape(peers, capacity, BLK, 2 * DH), "gy", split_axis=0, concat_axis=0, tiled=True
    ).reshape(slot_count, BLK, 2 * DH)

    proj_all = lax.all_gather(proj, ("gx", "gy"), axis=0, tiled=True)
    d_attended = dot_nt(cotangent, proj_all).astype(jnp.bfloat16)

    attended, grad_queries, grad_keys_local, grad_values_local, outgoing = attend(
        position, queries, keys_local, values_local, d_attended, returned
    )
    incoming = lax.all_to_all(
        outgoing.reshape(peers, capacity, BLK, 2 * DH), "gy", split_axis=0, concat_axis=0, tiled=True
    ).reshape(slot_count, BLK, 2 * DH)

    total_tokens = queries.shape[0] * sizes["gx"] * peers
    grad_proj = projection_gradient(attended, cotangent, sizes) * total_tokens ** (-0.5)
    mixed = jnp.dot(attended, proj_all, preferred_element_type=jnp.float32).astype(jnp.bfloat16)

    grad_mem_keys, grad_mem_values = collect_terms(wanted, incoming, peers, capacity)
    return (
        mixed,
        grad_proj,
        grad_queries,
        grad_keys_local,
        grad_values_local,
        grad_mem_keys,
        grad_mem_values,
    )


def solution(mesh):
    rows = P(("gx", "gy"), None)
    return jax.shard_map(
        functools.partial(local, dict(mesh.shape)),
        mesh=mesh,
        in_specs=(rows,) * 7 + (P(("gx", "gy"), None, None),),
        out_specs=(rows,) * 7,
        check_vma=False,
    )
```

time: 616 us -> 324 us (0.53)
  waiting for transfers between devices: 482 us -> 213 us
  matrix products: 59.8 us -> 18.3 us
  Pallas kernels: 0 us -> 32.1 us
  local copies, waits for them, and re-layouts: 35.3 us -> 9.1 us
  blocking collectives: 0 us -> 13.5 us
    reduce_scatter x1 -> x0, waiting for transfers between devices: 258 us -> none  [local(): lax.psum_scatter(lax.dot_general(columns, cotangent, (((0,), (0,)), ((),...]
    all_to_all x3 -> x2, waiting for transfers between devices: 223 us -> 1.76 us  [the longest x1 1.76 us: local(): lax.all_to_all(found.reshape(peers, capacity, BLK, 2 * DH), 'gy', split_a...]
    all_gather x1, waiting for transfers between devices: 0.02 us -> 118 us  [local(): proj_all = lax.all_gather(proj, ('gx', 'gy'), axis=0, tiled=True)]
    ppermute x0 -> x5, waiting for transfers between devices: none -> 93.2 us  [projection_gradient(): total = kept + lax.ppermute(sent, name, pairs).astype(jnp.float32)]
    dot_general x13 -> x4, matrix products: 59.8 us -> 18.3 us  [the longest x2 6.62 us: dot_tn(): lax.dot_general(a, b, (((0,), (0,)), ((), ())), preferred_element_type=jn...]
    pallas_call x0 -> x3, Pallas kernels: none -> 32.1 us  [the longest x1 17.9 us: attend(): pl.pallas_call(attention_kernel, out_shape=(rows, rows, rows, rows, jax.S...]
    unnamed x50 -> x17, local copies, waits for them, and re-layouts: 23.1 us -> 6.8 us
    all_to_all x0 -> x1, blocking collectives: none -> 13.5 us  [local(): lax.all_to_all(request.reshape(peers, capacity), 'gy', split_axis=0, conc...]
  transfers between devices with their start and end apart: 5 -> 8, of which waited for: 3 -> 6; matrix products, arithmetic and copies ran while one was open for 15% -> 8% of each run, Pallas kernels for 0% -> 4%
where the time goes in v1:
time: 324 us; the launch traced here: 323 us
  waiting for transfers between devices  213 us (66%)
  Pallas kernels  32.1 us (10%)
  matrix products  18.3 us (6%)
  starting transfers between devices  14.9 us (5%)
  between operations  14.2 us (4%)
  blocking collectives  13.5 us (4%)
  local copies, waits for them, and re-layouts  9.1 us (3%)
  other arithmetic  7.67 us (2%)
    all_gather x1, waiting for transfers between devices, local(): proj_all = lax.all_gather(proj, ('gx', 'gy'), axis=0, tiled=True)  118 us
    ppermute x5, waiting for transfers between devices, projection_gradient(): total = kept + lax.ppermute(sent, name, pairs).astype(jnp.float32)  93.2 us
    pallas_call x1, Pallas kernels, attend(): pl.pallas_call(attention_kernel, out_shape=(rows, rows, rows, rows, jax.S...  17.9 us
    all_to_all x1, blocking collectives, local(): lax.all_to_all(request.reshape(peers, capacity), 'gy', split_axis=0, conc...  13.5 us
    pallas_call x1, Pallas kernels, collect_terms(): pl.pallas_call(functools.partial(collect_kernel, capacity), out_shape=(ta...  9.23 us
    unnamed x17, local copies, waits for them, and re-layouts  6.8 us
    dot_general x2, matrix products, dot_tn(): lax.dot_general(a, b, (((0,), (0,)), ((), ())), preferred_element_type=jn...  6.62 us
  transfers between devices with their start and end apart: 8, of which 6 were waited for; matrix products, arithmetic and copies ran while one was open for 8% of the time, Pallas kernels for 4%

profile of v1, /device:TPU:0, one launch (start us, length us, event | category | flops | bytes accessed | tf_op | source)
XLA Modules:
  0.0 323.3 jit_solution(5228648494615467758)
XLA Ops:
  9.1 13.5 %all_to_all.16 = s32[8,1,8]{2,1,0:T(1,128)S(1)} all-to-all(s32[8,1,8]{2,1,0:T(1,128)S(1)} %bitcast.58), channel_id=1, replica_groups=mesh['gx'=4,'gy'=8] {'gy'}, dimensions={0} | all-to-all | bytes 512 | tf_op jit(solution)/shard_map/all_to_all | solution.py:212
  23.9 1.6 copy-done.1
  25.5 1.6 copy-done.2
  27.1 4.9 %shard_map.135 = bf16[64,128,256]{2,1,0:T(8,128)(2,1)} custom-call(s32[64]{0:T(128)S(1)} %reshape.181.wanted_ref, bf16[512,2048]{1,0:T(8,128)(2,1)S(1)} %copy-done.1, bf16[512,2048]{1,0:T(8,128)(2,1)S(1)} %copy-done.2), custom_call_target="tpu_custom_call" | custom-call | tf_op jit(solution)/shard_map/pallas_call | solution.py:43
  32.0 4.6 %all-to-all-start.1 = ((bf16[8,8,128,256]{3,2,1,0:T(8,128)(2,1)}), bf16[8,8,128,256]{3,2,1,0:T(8,128)(2,1)}, u32[]{:S(2)}, u32[]{:S(2)}) async-start(bf16[8,8,128,256]{3,2,1,0:T(8,128)(2,1)} %bitcast.53), calls=%async_computation.1 | async-start | bytes 8388608 | tf_op jit(solution)/shard_map/all_to_all | solution.py:217
  36.6 117.8 %all-gather.2.cloned.1.call-done = bf16[2048,2048]{1,0:T(8,128)(2,1)} async-done(((bf16[64,2048]{1,0:T(8,128)(2,1)}), bf16[2048,2048]{1,0:T(8,128)(2,1)}) %all-gather.2.cloned.1.call-update) | async-done | bytes 8388624 | tf_op jit(solution)/shard_map/all_gather | solution.py:221
  154.4 6.3 %convolution_convert_fusion.2.do_ref = bf16[128,2048]{1,0:T(8,128)(2,1)S(1)} fusion(bf16[128,2048]{1,0:T(8,128)(2,1)S(1)} %copy-done, bf16[2048,2048]{1,0:T(8,128)(2,1)} %all-gather.2.cloned.1.call-done), kind=kOutput, calls=%fused_computation.5 | convolution fusion | flops 1074003968 | bytes 9437184 | tf_op jit(solution)/shard_map/dot_general | solution.py:57
  160.7 1.8 all-to-all-done.1
  162.5 17.9 %shard_map.136 = (bf16[128,2048]{1,0:T(8,128)(2,1)S(1)}, bf16[128,2048]{1,0:T(8,128)(2,1)}, bf16[128,2048]{1,0:T(8,128)(2,1)}, bf16[128,2048]{1,0:T(8,128)(2,1)}, bf16[64,128,256]{2,1,0:T(8,128)(2,1)}) custom-call(s32[48]{0:T(128)S(1)} %multiply_add_fusion.position_ref, bf16[128,2048]{1,0:T(8,128)(2,1)S(1)} %copy-done.3, bf16[128,2048]{1,0:T(8,128)(2,1)S(1)} %copy-done.4, ...), custom_call_target="tpu_custom_call" | custom-call | tf_op jit(solution)/shard_map/pallas_call | solution.py:108
  180.7 3.2 convolution_convert_fusion
  183.9 4.6 %all-to-all-start.2 = ((bf16[8,8,128,256]{3,2,1,0:T(8,128)(2,1)}), bf16[8,8,128,256]{3,2,1,0:T(8,128)(2,1)}, u32[]{:S(2)}, u32[]{:S(2)}) async-start(bf16[8,8,128,256]{3,2,1,0:T(8,128)(2,1)} %bitcast.54), calls=%async_computation.2 | async-start | bytes 8388608 | tf_op jit(solution)/shard_map/all_to_all | solution.py:227
  188.5 2.9 collective-permute-done
  191.4 3.4 %add_convert_fusion = bf16[2,2,2,2,64,2048]{5,4,3,2,1,0:T(8,128)(2,1)S(1)} fusion(bf16[2,2,2,2,64,2048]{5,4,3,2,1,0:T(8,128)(2,1)} %collective-permute-done, bf16[128,2048]{1,0:T(8,128)(2,1)S(1)} %copy-done, bf16[128,2,2,2,2,2,64]{0,6,5,4,3,2,1:T(8,128)(2,1)S(1)} %bitcast.56, s32[]{:T(128)S(6)} %select_n.78), kind=kOutput, calls=%fused_computation | convolution fusion | flops 543162368 | bytes 9175044 | tf_op jit(solution)/shard_map/dot_general | solution.py:61
  194.9 1.9 copy-done.6
  196.9 1.6 collective-permute-start.1
  198.5 46.3 %collective-permute-done.1 = bf16[2,2,2,64,2048]{4,3,2,1,0:T(8,128)(2,1)} collective-permute-done((bf16[2,2,2,64,2048]{4,3,2,1,0:T(8,128)(2,1)S(1)}, bf16[2,2,2,64,2048]{4,3,2,1,0:T(8,128)(2,1)}, u32[]{:S(2)}, u32[]{:S(2)}) %collective-permute-start.1) | collective-permute-done | bytes 2097184 | tf_op jit(solution)/shard_map/ppermute | solution.py:193
  244.8 3.0 fusion
  248.8 1.4 collective-permute-start.2
  250.3 32.4 %collective-permute-done.2 = bf16[2,2,64,2048]{3,2,1,0:T(8,128)(2,1)} collective-permute-done((bf16[2,2,64,2048]{3,2,1,0:T(8,128)(2,1)}, bf16[2,2,64,2048]{3,2,1,0:T(8,128)(2,1)}, u32[]{:S(2)}, u32[]{:S(2)}) %collective-permute-start.2) | collective-permute-done | bytes 1048608 | tf_op jit(solution)/shard_map/ppermute | solution.py:193
  282.6 1.6 fusion.1
  286.0 11.6 %collective-permute-done.3 = bf16[2,64,2048]{2,1,0:T(8,128)(2,1)S(1)} collective-permute-done((bf16[2,64,2048]{2,1,0:T(8,128)(2,1)S(1)}, bf16[2,64,2048]{2,1,0:T(8,128)(2,1)S(1)}, u32[]{:S(2)}, u32[]{:S(2)}) %collective-permute-start.3) | collective-permute-done | bytes 524320 | tf_op jit(solution)/shard_map/ppermute | solution.py:193
  298.8 2.1 collective-permute-start.4
  300.9 5.5 %convolution_convert_fusion.1 = bf16[128,2048]{1,0:T(8,128)(2,1)} fusion(bf16[128,2048]{1,0:T(8,128)(2,1)S(1)} %get-tuple-element.14, bf16[2048,2048]{1,0:T(8,128)(2,1)} %all-gather.2.cloned.1.call-done), kind=kOutput, calls=%fused_computation.4 | convolution fusion | flops 1074003968 | bytes 9437184 | tf_op jit(solution)/shard_map/dot_general | solution.py:233
  306.4 9.2 %shard_map.137 = (bf16[512,2048]{1,0:T(8,128)(2,1)}, bf16[512,2048]{1,0:T(8,128)(2,1)}) custom-call(s32[64]{0:T(128)S(1)} %reshape.181.wanted_ref, bf16[64,128,256]{2,1,0:T(8,128)(2,1)} %bitcast.21.incoming_ref), custom_call_target="tpu_custom_call" | custom-call | tf_op jit(solution)/shard_map/pallas_call | solution.py:152
  (38 shorter events, 8.4 us)
Async XLA Ops:
  7.2 147.3 %copy-start = (bf16[128,2048]{1,0:T(8,128)(2,1)S(1)}, bf16[128,2048]{1,0:T(8,128)(2,1)}, u32[]{:S(2)}) copy-start(bf16[128,2048]{1,0:T(8,128)(2,1)} %param.14) | copy-start | bytes 1572868
  7.2 147.3 %all-gather.2.cloned.1.call-start = ((), (), s32[]{:S(2)}) async-start(), calls=%async_computation.3 | async-start | bytes 8650752 | tf_op jit(solution)/shard_map/all_gather | solution.py:221
  23.9 1.6 copy-start.1
  25.5 1.6 copy-start.2
  32.0 130.5 %all-to-all-start.1 = ((bf16[8,8,128,256]{3,2,1,0:T(8,128)(2,1)}), bf16[8,8,128,256]{3,2,1,0:T(8,128)(2,1)}, u32[]{:S(2)}, u32[]{:S(2)}) async-start(bf16[8,8,128,256]{3,2,1,0:T(8,128)(2,1)} %bitcast.53), calls=%async_computation.1 | async-start | bytes 8388608 | tf_op jit(solution)/shard_map/all_to_all | solution.py:217
  36.6 125.9 %copy-start.3 = (bf16[128,2048]{1,0:T(8,128)(2,1)S(1)}, bf16[128,2048]{1,0:T(8,128)(2,1)}, u32[]{:S(2)}) copy-start(bf16[128,2048]{1,0:T(8,128)(2,1)} %q_ref.1) | copy-start | bytes 1572868
  36.6 125.9 %copy-start.4 = (bf16[128,2048]{1,0:T(8,128)(2,1)S(1)}, bf16[128,2048]{1,0:T(8,128)(2,1)}, u32[]{:S(2)}) copy-start(bf16[128,2048]{1,0:T(8,128)(2,1)} %k_ref.1) | copy-start | bytes 1572868
  36.6 125.9 %copy-start.5 = (bf16[128,2048]{1,0:T(8,128)(2,1)S(1)}, bf16[128,2048]{1,0:T(8,128)(2,1)}, u32[]{:S(2)}) copy-start(bf16[128,2048]{1,0:T(8,128)(2,1)} %v_ref.1) | copy-start | bytes 1572868
  183.9 7.5 %collective-permute-start = (bf16[2,2,2,2,64,2048]{5,4,3,2,1,0:T(8,128)(2,1)}, bf16[2,2,2,2,64,2048]{5,4,3,2,1,0:T(8,128)(2,1)}, u32[]{:S(2)}, u32[]{:S(2)}) collective-permute-start(bf16[2,2,2,2,64,2048]{5,4,3,2,1,0:T(8,128)(2,1)} %bitcast.11), channel_id=1, source_target_pairs={{0,8},{8,0},{16,24},{24,16},{1,9},{9,1},{17,25},{25,17},{2,10},{10... | collective-permute-start | bytes 12582920 | tf_op jit(solution)/shard_map/ppermute | solution.py:193
  183.9 122.5 %all-to-all-start.2 = ((bf16[8,8,128,256]{3,2,1,0:T(8,128)(2,1)}), bf16[8,8,128,256]{3,2,1,0:T(8,128)(2,1)}, u32[]{:S(2)}, u32[]{:S(2)}) async-start(bf16[8,8,128,256]{3,2,1,0:T(8,128)(2,1)} %bitcast.54), calls=%async_computation.2 | async-start | bytes 8388608 | tf_op jit(solution)/shard_map/all_to_all | solution.py:227
  194.9 1.9 copy-start.6
  196.9 47.8 %collective-permute-start.1 = (bf16[2,2,2,64,2048]{4,3,2,1,0:T(8,128)(2,1)S(1)}, bf16[2,2,2,64,2048]{4,3,2,1,0:T(8,128)(2,1)}, u32[]{:S(2)}, u32[]{:S(2)}) collective-permute-start(bf16[2,2,2,64,2048]{4,3,2,1,0:T(8,128)(2,1)S(1)} %dynamic-slice_bitcast_fusion), channel_id=1, source_target_pairs={{0,16},{8,24},{16,0},{24,8},{1,17},{9,25},{17,1},{25,9},{2,18},{10... | collective-permute-start | bytes 6291464 | tf_op jit(solution)/shard_map/ppermute | solution.py:193
  248.8 33.8 %collective-permute-start.2 = (bf16[2,2,64,2048]{3,2,1,0:T(8,128)(2,1)}, bf16[2,2,64,2048]{3,2,1,0:T(8,128)(2,1)}, u32[]{:S(2)}, u32[]{:S(2)}) collective-permute-start(bf16[2,2,64,2048]{3,2,1,0:T(8,128)(2,1)} %dynamic-slice_bitcast_fusion.1), channel_id=1, source_target_pairs={{0,1},{1,0},{2,3},{3,2},{4,5},{5,4},{6,7},{7,6},{8,9},{9,8},{10,11... | collective-permute-start | bytes 3145736 | tf_op jit(solution)/shard_map/ppermute | solution.py:193
  284.3 1.0 copy-start.7
  285.3 12.3 %collective-permute-start.3 = (bf16[2,64,2048]{2,1,0:T(8,128)(2,1)S(1)}, bf16[2,64,2048]{2,1,0:T(8,128)(2,1)S(1)}, u32[]{:S(2)}, u32[]{:S(2)}) collective-permute-start(bf16[2,64,2048]{2,1,0:T(8,128)(2,1)S(1)} %dynamic-slice_bitcast_fusion.2), channel_id=1, source_target_pairs={{0,2},{1,3},{2,0},{3,1},{4,6},{5,7},{6,4},{7,5},{8,10},{9,11},{10,... | collective-permute-start | bytes 1572872 | tf_op jit(solution)/shard_map/ppermute | solution.py:193
  298.8 16.8 %collective-permute-start.4 = (bf16[64,2048]{1,0:T(8,128)(2,1)S(1)}, bf16[64,2048]{1,0:T(8,128)(2,1)S(1)}, u32[]{:S(2)}, u32[]{:S(2)}) collective-permute-start(bf16[64,2048]{1,0:T(8,128)(2,1)S(1)} %dynamic-slice_bitcast_fusion.3), channel_id=1, source_target_pairs={{0,4},{1,5},{2,6},{3,7},{4,0},{5,1},{6,2},{7,3},{8,12},{9,13},{10,... | collective-permute-start | bytes 786440 | tf_op jit(solution)/shard_map/ppermute | solution.py:193
Sparse Core Ops, SparseCore 0:
  11.0 143.4 all-gather.1
